TPU v7x, 32 devices: a whole 2x2x4 slice. The times are simulated.
32 devices in a mesh: seq: 4 (over z), dp: 8 (over y, x, core).
Axes of the slice: x: 2, y: 2, z: 4, core: 2. Of those that a mesh axis runs over, the one named last changes fastest.
Arguments:
- tokens: bfloat16 [8, 1024, 768], P('dp', 'seq'), may hold values from -6 to 6
- qkv_weight: bfloat16 [768, 2304], P('dp'), may hold values from -0.21875 to 0.21875
- proj_weight: bfloat16 [768, 768], P('dp'), may hold values from -0.875 to 0.875
- hidden_weight: bfloat16 [768, 3072], P('dp'), may hold values from -0.21875 to 0.21875
- output_weight: bfloat16 [3072, 768], P('dp'), may hold values from -0.109375 to 0.109375
- first_gain: bfloat16 [768], P('dp'), may hold values from 0.25 to 1.75
- first_bias: bfloat16 [768], P('dp'), may hold values from -2.5 to 2.5
- second_gain: bfloat16 [768], P('dp'), may hold values from 0.25 to 1.75
- second_bias: bfloat16 [768], P('dp'), may hold values from -2.5 to 2.5
- cotangent: bfloat16 [8, 1024, 768], P('dp', 'seq'), may hold values from -6 to 6
Outputs:
- block_out: bfloat16 [8, 1024, 768], P('dp', 'seq')
- tokens_gradient: bfloat16 [8, 1024, 768], P('dp', 'seq')
- qkv_gradient: float32 [768, 2304], P('dp')
- proj_gradient: float32 [768, 768], P('dp')
- hidden_gradient: float32 [768, 3072], P('dp')
- output_gradient: float32 [3072, 768], P('dp')
- first_gain_gradient: float32 [768], P('dp')
- first_bias_gradient: float32 [768], P('dp')
- second_gain_gradient: float32 [768], P('dp')
- second_bias_gradient: float32 [768], P('dp')
All inputs are finite; a program needn't handle non-finite values.
Results may differ from a plain program's by a relative error of at most 0.012.
Values may be sent and summed in bfloat16 or wider, within the bound.
A program may use at most 256 MiB of HBM per device.

v0:
```python
import jax
import jax.numpy as jnp
from jax import lax
from jax.sharding import PartitionSpec as P

HEAD_DIM = 64
LOW = jnp.bfloat16
F32 = jnp.float32


def layer_norm(values, gain, bias):
    average = jnp.mean(values, -1, keepdims=True)
    centred = values - average
    variance = jnp.mean(centred * centred, -1, keepdims=True)
    return centred * lax.rsqrt(variance + 1e-05) * gain + bias


def gelu_tanh(values):
    return jax.nn.gelu(values, approximate=True)


def matmul(left, right):
    return jnp.dot(left, right, preferred_element_type=F32)


def matmul_left_t(left, right):
    return lax.dot_general(left, right, (((0,), (0,)), ((), ())), preferred_element_type=F32)


def matmul_right_t(left, right):
    return lax.dot_general(left, right, (((1,), (1,)), ((), ())), preferred_element_type=F32)


def gather_seq(value):
    return lax.all_gather(value, "seq", axis=0, tiled=True)


def scatter_seq(value):
    return lax.psum_scatter(value.astype(LOW), "seq", scatter_dimension=0, tiled=True).astype(F32)


def attention_forward(queries, keys, values):
    length, local_width = queries.shape
    heads_here = local_width // HEAD_DIM
    block_rows = min(512, length)
    blocks = length // block_rows
    scale = HEAD_DIM ** (-0.5)
    outs, logs = ([], [])
    key_index = jnp.arange(length)
    for b in range(blocks):
        seen = (b + 1) * block_rows
        q = queries[b * block_rows : seen].reshape(block_rows, heads_here, HEAD_DIM)
        k = keys[:seen].reshape(seen, heads_here, HEAD_DIM)
        v = values[:seen].reshape(seen, heads_here, HEAD_DIM)
        raw = jnp.einsum("qhd,khd->hqk", q, k, preferred_element_type=F32)
        positions = b * block_rows + jnp.arange(block_rows)
        causal = key_index[None, :seen] <= positions[:, None]
        scores = jnp.where(causal[None], raw * scale, -1e30)
        largest = jnp.max(scores, -1, keepdims=True)
        expo = jnp.exp(scores - largest)
        total = jnp.sum(expo, -1, keepdims=True)
        probs = (expo / total).astype(LOW)
        context = jnp.einsum("hqk,khd->qhd", probs, v, preferred_element_type=F32)
        outs.append(context.astype(LOW).reshape(block_rows, local_width))
        logs.append(largest + jnp.log(total))
    return (jnp.concatenate(outs, axis=0), logs)


def attention_backward(queries, keys, values, grads, logs):
    length, local_width = queries.shape
    heads_here = local_width // HEAD_DIM
    block_rows = min(512, length)
    blocks = length // block_rows
    scale = HEAD_DIM ** (-0.5)
    key_index = jnp.arange(length)
    query_grads = []
    key_sum = jnp.zeros((length, heads_here, HEAD_DIM), F32)
    value_sum = jnp.zeros((length, heads_here, HEAD_DIM), F32)
    for b in range(blocks):
        seen = (b + 1) * block_rows
        q = queries[b * block_rows : seen].reshape(block_rows, heads_here, HEAD_DIM)
        g = grads[b * block_rows : seen].reshape(block_rows, heads_here, HEAD_DIM)
        k = keys[:seen].reshape(seen, heads_here, HEAD_DIM)
        v = values[:seen].reshape(seen, heads_here, HEAD_DIM)
        raw = jnp.einsum("qhd,khd->hqk", q, k, preferred_element_type=F32)
        positions = b * block_rows + jnp.arange(block_rows)
        causal = key_index[None, :seen] <= positions[:, None]
        scores = jnp.where(causal[None], raw * scale, -1e30)
        probs = jnp.exp(scores - logs[b])
        low_probs = probs.astype(LOW)
        value_term = jnp.einsum("hqk,qhd->khd", low_probs, g, preferred_element_type=F32)
        prob_grad = jnp.einsum("qhd,khd->hqk", g, v, preferred_element_type=F32)
        score_grad = (probs * (prob_grad - jnp.sum(probs * prob_grad, -1, keepdims=True))).astype(
            LOW
        )
        query_grad = jnp.einsum("hqk,khd->qhd", score_grad, k, preferred_element_type=F32) * scale
        key_term = jnp.einsum("hqk,qhd->khd", score_grad, q, preferred_element_type=F32) * scale
        pad = ((0, length - seen), (0, 0), (0, 0))
        key_sum = key_sum + jnp.pad(key_term, pad)
        value_sum = value_sum + jnp.pad(value_term, pad)
        query_grads.append(query_grad.astype(LOW).reshape(block_rows, local_width))
    return (
        jnp.concatenate(query_grads, axis=0),
        key_sum.astype(LOW).reshape(length, local_width),
        value_sum.astype(LOW).reshape(length, local_width),
    )


def on_device(
    tokens,
    qkv_weight,
    proj_weight,
    hidden_weight,
    output_weight,
    first_gain,
    first_bias,
    second_gain,
    second_bias,
    cotangent,
):
    parts = lax.axis_size("seq")
    groups = lax.axis_size("dp")
    part = lax.axis_index("seq")
    inputs_low = tokens[0]
    rows, width = inputs_low.shape
    model_rows = qkv_weight.shape[0]
    local_width = width // parts
    hidden_rows = output_weight.shape[0] // parts
    hidden_here = hidden_rows * groups
    qkv_here = lax.dynamic_index_in_dim(
        qkv_weight.reshape(model_rows, 3, parts, local_width), part, 2, keepdims=False
    ).reshape(model_rows, 3 * local_width)
    hidden_cols = lax.dynamic_index_in_dim(
        hidden_weight.reshape(model_rows, groups, parts, hidden_rows), part, 2, keepdims=False
    ).reshape(model_rows, hidden_here)
    output_here = lax.dynamic_slice_in_dim(output_weight, part * hidden_rows, hidden_rows, 0)
    norms = jnp.stack([first_gain, first_bias, second_gain, second_bias], axis=0)
    norms = lax.all_gather(norms, "dp", axis=1, tiled=True).astype(F32)
    gain_one, bias_one, gain_two, bias_two = (norms[0], norms[1], norms[2], norms[3])
    all_tokens = gather_seq(inputs_low)
    wide_qkv = lax.all_gather(qkv_here, "dp", axis=0, tiled=True)
    wide_proj = lax.all_gather(proj_weight, "dp", axis=0, tiled=True)
    wide_hidden = lax.all_gather(hidden_cols, "dp", axis=0, tiled=True)
    wide_output = lax.all_gather(output_here, "dp", axis=0, tiled=True)
    all_grads = gather_seq(cotangent[0])
    inputs = all_tokens.astype(F32)
    lowered_one = layer_norm(inputs, gain_one, bias_one).astype(LOW)
    projected = matmul(lowered_one, wide_qkv).astype(LOW)
    queries = projected[:, :local_width]
    keys = projected[:, local_width : 2 * local_width]
    values = projected[:, 2 * local_width :]
    context_here, logs = attention_forward(queries, keys, values)
    context = lax.all_gather(context_here, "seq", axis=1, tiled=True)
    middle = inputs + matmul(context, wide_proj)
    lowered_two = layer_norm(middle, gain_two, bias_two).astype(LOW)
    hidden_pre = matmul(lowered_two, wide_hidden)
    activated_float, gelu_pull = jax.vjp(gelu_tanh, hidden_pre)
    activated = activated_float.astype(LOW)
    act_grad = matmul_right_t(all_grads, wide_output)
    pre_grad = gelu_pull(act_grad)[0].astype(LOW)
    normed_two_grad = scatter_seq(matmul_right_t(pre_grad, wide_hidden))
    ffn_out = scatter_seq(matmul(activated, wide_output))
    middle_own = lax.dynamic_slice_in_dim(middle, part * rows, rows, 0)
    block_out = middle_own + ffn_out
    _, norm_pull_two = jax.vjp(layer_norm, middle_own, gain_two, bias_two)
    middle_part, gain_two_term, bias_two_term = norm_pull_two(normed_two_grad)
    middle_grad = cotangent[0].astype(F32) + middle_part
    attn_grad = gather_seq(middle_grad.astype(LOW))
    proj_here = lax.dynamic_slice_in_dim(wide_proj, part * local_width, local_width, 0)
    context_grad = matmul_right_t(attn_grad, proj_here).astype(LOW)
    query_grads, key_grads, value_grads = attention_backward(
        queries, keys, values, context_grad, logs
    )
    qkv_grad = jnp.concatenate([query_grads, key_grads, value_grads], axis=1)
    normed_one_grad = scatter_seq(matmul_right_t(qkv_grad, wide_qkv))
    _, norm_pull_one = jax.vjp(layer_norm, inputs_low.astype(F32), gain_one, bias_one)
    input_part, gain_one_term, bias_one_term = norm_pull_one(normed_one_grad)
    tokens_gradient = (middle_grad + input_part).astype(LOW)
    attn_cols = lax.dynamic_slice_in_dim(attn_grad, part * local_width, local_width, 1)
    output_term = matmul_left_t(activated, all_grads).astype(LOW)
    hidden_term = matmul_left_t(lowered_two, pre_grad).astype(LOW)
    proj_term = matmul_left_t(context, attn_cols).astype(LOW)
    qkv_term = matmul_left_t(lowered_one, qkv_grad).astype(LOW)
    first_terms = jnp.concatenate([output_term, hidden_term], axis=1)
    second_terms = jnp.concatenate([proj_term, qkv_term], axis=1)
    first_sum = lax.psum_scatter(first_terms, "dp", scatter_dimension=0, tiled=True)
    second_sum = lax.psum_scatter(second_terms, "dp", scatter_dimension=0, tiled=True)
    first_all = lax.all_gather(first_sum, "seq", axis=0)
    second_all = lax.all_gather(second_sum, "seq", axis=0)
    output_gradient = first_all[:, :, :width].reshape(parts * hidden_rows, width).astype(F32)
    hidden_gradient = (
        first_all[:, :, width:]
        .reshape(parts, model_rows, groups, hidden_rows)
        .transpose(1, 2, 0, 3)
        .reshape(model_rows, parts * hidden_here)
        .astype(F32)
    )
    proj_gradient = (
        second_all[:, :, :local_width].transpose(1, 0, 2).reshape(model_rows, width).astype(F32)
    )
    qkv_gradient = (
        second_all[:, :, local_width:]
        .reshape(parts, model_rows, 3, local_width)
        .transpose(1, 2, 0, 3)
        .reshape(model_rows, 3 * width)
        .astype(F32)
    )
    norm_terms = jnp.stack([gain_one_term, bias_one_term, gain_two_term, bias_two_term], axis=0)
    norm_sum = lax.psum(norm_terms, ("seq", "dp"))
    norm_own = lax.dynamic_slice_in_dim(
        norm_sum, lax.axis_index("dp") * first_gain.shape[0], first_gain.shape[0], 1
    )
    return (
        block_out.astype(LOW)[None],
        tokens_gradient[None],
        qkv_gradient,
        proj_gradient,
        hidden_gradient,
        output_gradient,
        norm_own[0],
        norm_own[1],
        norm_own[2],
        norm_own[3],
    )


def solution(mesh):
    placed = (
        P("dp", "seq", None),
        P("dp", None),
        P("dp", None),
        P("dp", None),
        P("dp", None),
        P("dp"),
        P("dp"),
        P("dp"),
        P("dp"),
        P("dp", "seq", None),
    )
    return jax.shard_map(
        on_device,
        mesh=mesh,
        in_specs=placed,
        out_specs=(
            P("dp", "seq", None),
            P("dp", "seq", None),
            P("dp", None),
            P("dp", None),
            P("dp", None),
            P("dp", None),
            P("dp"),
            P("dp"),
            P("dp"),
            P("dp"),
        ),
        check_vma=False,
    )
```

profile of v0, /device:TPU:0, one launch (start us, length us, event | category | flops | bytes accessed | tf_op | source)
XLA Modules:
  0.0 499.9 jit_solution(855848961846258834)
XLA Ops:
  10.8 10.3 %all-gather.4 = bf16[8,96,4]{1,2,0:T(4,128)(2,1)S(1)} all-gather(bf16[1,96,4]{1,2,0:T(4,128)(2,1)S(1)} %maximum_bitcast_fusion), channel_id=1, replica_groups=mesh['seq'=4,'dp'=8] {'dp'}, dimensions={0}, use_global_device_ids=true | all-gather | bytes 6912 | tf_op jit(solution)/shard_map/all_gather | solution.py:138
  24.7 11.9 %all_gather.41 = bf16[768,576]{1,0:T(8,128)(2,1)} all-gather(bf16[96,576]{1,0:T(8,128)(2,1)S(1)} %copy.126), channel_id=1, replica_groups=mesh['seq'=4,'dp'=8] {'dp'}, dimensions={0}, use_global_device_ids=true | all-gather | bytes 995328 | tf_op jit(solution)/shard_map/all_gather | solution.py:141
  36.7 13.9 %all-gather.24.cloned.1.call-done = bf16[1,1024,768]{1,2,0:T(8,128)(2,1)} async-done(((bf16[1,256,768]{1,2,0:T(8,128)(2,1)}), bf16[1,1024,768]{1,2,0:T(8,128)(2,1)}) %all-gather.24.cloned.1.call-update) | async-done | bytes 1572880 | tf_op jit(solution)/shard_map/all_gather | solution.py:35
  69.1 5.8 %all-gather.16.cloned.1.call-done = bf16[768,768]{1,0:T(8,128)(2,1)} async-done(((bf16[96,768]{1,0:T(8,128)(2,1)}), bf16[768,768]{1,0:T(8,128)(2,1)}) %all-gather.16.cloned.1.call-update) | async-done | bytes 1179664 | tf_op jit(solution)/shard_map/all_gather | solution.py:142
  74.8 39.3 %all-gather.14.cloned.1.call-done = bf16[1024,768]{0,1:T(8,128)(2,1)} async-done(((bf16[1024,192]{0,1:T(8,128)(2,1)}), bf16[1024,768]{0,1:T(8,128)(2,1)}) %all-gather.14.cloned.1.call-update) | async-done | bytes 1572880 | tf_op jit(solution)/shard_map/all_gather | solution.py:153
  114.1 3.7 fusion.90
  120.2 19.2 %all-gather.18.cloned.1.call-done = bf16[768,768]{1,0:T(8,128)(2,1)} async-done(((bf16[96,768]{1,0:T(8,128)(2,1)}), bf16[768,768]{1,0:T(8,128)(2,1)}) %all-gather.18.cloned.1.call-update) | async-done | bytes 1179664 | tf_op jit(solution)/shard_map/all_gather | solution.py:143
  139.4 4.8 fusion.91
  144.2 21.0 %all-gather.20.cloned.1.call-done = bf16[768,768]{1,0:T(8,128)(2,1)} async-done(((bf16[96,768]{1,0:T(8,128)(2,1)}), bf16[768,768]{1,0:T(8,128)(2,1)}) %all-gather.20.cloned.1.call-update) | async-done | bytes 1179664 | tf_op jit(solution)/shard_map/all_gather | solution.py:144
  165.2 38.5 %all-gather.26.cloned.1.call-done = bf16[1,1024,768]{2,1,0:T(8,128)(2,1)} async-done(((bf16[1,256,768]{2,1,0:T(8,128)(2,1)}), bf16[1,1024,768]{2,1,0:T(8,128)(2,1)}) %all-gather.26.cloned.1.call-update) | async-done | bytes 1572880 | tf_op jit(solution)/shard_map/all_gather | solution.py:35
  203.8 5.6 %fusion.16 = bf16[1024,768]{1,0:T(8,128)(2,1)S(1)} fusion(f32[1024,768]{1,0:T(8,128)} %fusion.91, bf16[768,768]{1,0:T(8,128)(2,1)} %all-gather.20.cloned.1.call-done, bf16[1,1024,768]{2,1,0:T(8,128)(2,1)} %all-gather.26.cloned.1.call-done), kind=kOutput, calls=%fused_computation.26 | convolution fusion | flops 1223688192 | bytes 7471104 | tf_op jit(solution)/shard_map/dot_general | solution.py:31
  213.4 3.5 convolution_convert_fusion.3
  220.2 4.3 copy.156
  227.2 20.3 %reduce-scatter.12.cloned.1.call-done = bf16[256,768]{0,1:T(8,128)(2,1)} async-done(((bf16[1024,768]{0,1:T(8,128)(2,1)}), bf16[256,768]{0,1:T(8,128)(2,1)}) %reduce-scatter.12.cloned.1.call-update) | async-done | bytes 393232 | tf_op jit(solution)/shard_map/reduce_scatter | solution.py:39
  252.2 2.7 fusion.70
  257.0 35.3 %reduce-scatter.18.cloned.1.call-done = bf16[96,1536]{1,0:T(8,128)(2,1)} async-done(((bf16[768,1536]{1,0:T(8,128)(2,1)}), bf16[96,1536]{1,0:T(8,128)(2,1)}) %reduce-scatter.18.cloned.1.call-update) | async-done | bytes 294928 | tf_op jit(solution)/shard_map/reduce_scatter | solution.py:186
  292.4 39.9 %all-gather.22.cloned.1.call-done = bf16[1024,768]{0,1:T(8,128)(2,1)} async-done(((bf16[256,768]{0,1:T(8,128)(2,1)}), bf16[1024,768]{0,1:T(8,128)(2,1)}) %all-gather.22.cloned.1.call-update) | async-done | bytes 1572880 | tf_op jit(solution)/shard_map/all_gather | solution.py:35
  354.3 5.0 %convolution_convert_fusion.2 = bf16[1024,768]{0,1:T(8,128)(2,1)} fusion(bf16[768,768]{1,0:T(8,128)(2,1)} %all-gather.20.cloned.1.call-done, f32[1024,768]{1,0:T(8,128)} %fusion.91), kind=kOutput, calls=%fused_computation.50 | convolution fusion | flops 1215823872 | bytes 5898240 | tf_op jit(solution)/shard_map/dot_general | solution.py:23
  369.0 3.6 reshape.282
  373.8 28.3 %reduce-scatter.16.cloned.1.call-done = bf16[96,768]{1,0:T(8,128)(2,1)} async-done(((bf16[768,768]{1,0:T(8,128)(2,1)}), bf16[96,768]{1,0:T(8,128)(2,1)}) %reduce-scatter.16.cloned.1.call-update) | async-done | bytes 147472 | tf_op jit(solution)/shard_map/reduce_scatter | solution.py:187
  402.0 22.2 %all-gather.2 = bf16[384,768]{1,0:T(8,128)(2,1)S(1)} all-gather(bf16[96,768]{1,0:T(8,128)(2,1)} %reduce-scatter.16.cloned.1.call-done), channel_id=4, replica_groups=mesh['seq'=4,'dp'=8] {'seq'}, dimensions={0}, use_global_device_ids=true | all-gather | bytes 737280 | tf_op jit(solution)/shard_map/all_gather | solution.py:189
  427.8 2.9 reshape.280
  430.7 13.6 %reduce-scatter.14.cloned.1.call-done = bf16[256,768]{0,1:T(8,128)(2,1)} async-done(((bf16[1024,768]{0,1:T(8,128)(2,1)}), bf16[256,768]{0,1:T(8,128)(2,1)}) %reduce-scatter.14.cloned.1.call-update) | async-done | bytes 393232 | tf_op jit(solution)/shard_map/reduce_scatter | solution.py:39
  447.3 41.4 %psum.7 = f32[4,768]{1,0:T(4,128)S(1)} all-reduce(f32[4,768]{1,0:T(4,128)S(1)} %pad_maximum_fusion.6), channel_id=1, replica_groups=mesh['seq'=4,'dp'=8] {'seq','dp'}, use_global_device_ids=true, to_apply=%region_27.28 | all-reduce | flops 3072 | bytes 24576 | tf_op jit(solution)/shard_map/psum | solution.py:209
  (236 shorter events, 87.7 us)
Async XLA Ops:
  7.2 60.5 %copy-start = (bf16[384,768]{1,0:T(8,128)(2,1)S(1)}, bf16[384,768]{1,0:T(8,128)(2,1)}, u32[]{:S(2)}) copy-start(bf16[384,768]{1,0:T(8,128)(2,1)} %param.14) | copy-start | bytes 1769476
  7.2 43.4 %all-gather.24.cloned.1.call-start = ((), (), s32[]{:S(2)}) async-start(), calls=%async_computation.13 | async-start | bytes 1966080 | tf_op jit(solution)/shard_map/all_gather | solution.py:35
  9.2 65.6 %all-gather.16.cloned.1.call-start = ((), (), s32[]{:S(2)}) async-start(), calls=%async_computation.6 | async-start | bytes 1327104 | tf_op jit(solution)/shard_map/all_gather | solution.py:142
  10.0 104.1 %all-gather.14.cloned.1.call-start = ((), (), s32[]{:S(2)}) async-start(), calls=%async_computation.5 | async-start | bytes 1966080 | tf_op jit(solution)/shard_map/all_gather | solution.py:153
  21.8 32.5 %copy-start.47 = (f32[768]{0:T(1024)}, f32[768]{0:T(1024)S(1)}, u32[]{:S(2)}) copy-start(f32[768]{0:T(1024)S(1)} %get-tuple-element.82) | copy-start | bytes 9220
  64.2 75.2 %all-gather.18.cloned.1.call-start = ((), (), s32[]{:S(2)}) async-start(), calls=%async_computation.7 | async-start | bytes 1327104 | tf_op jit(solution)/shard_map/all_gather | solution.py:143
  67.6 97.6 %all-gather.20.cloned.1.call-start = ((), (), s32[]{:S(2)}) async-start(), calls=%async_computation.8 | async-start | bytes 1327104 | tf_op jit(solution)/shard_map/all_gather | solution.py:144
  68.4 135.3 %all-gather.26.cloned.1.call-start = ((), (), s32[]{:S(2)}) async-start(), calls=%async_computation.14 | async-start | bytes 1966080 | tf_op jit(solution)/shard_map/all_gather | solution.py:35
  69.0 178.5 %reduce-scatter.12.cloned.1.call-start = ((), (), s32[]{:S(2)}) async-start(), calls=%async_computation.10 | async-start | bytes 1966080 | tf_op jit(solution)/shard_map/reduce_scatter | solution.py:39
  117.9 131.6 %copy-start.5 = (f32[1024,768]{0,1:T(8,128)}, f32[1024,768]{0,1:T(8,128)S(1)}, u32[]{:S(2)}) copy-start(f32[1024,768]{0,1:T(8,128)S(1)} %get-tuple-element.109) | copy-start | bytes 9437188
  213.2 79.1 %reduce-scatter.18.cloned.1.call-start = ((), (), s32[]{:S(2)}) async-start(), calls=%async_computation.17 | async-start | bytes 2654208 | tf_op jit(solution)/shard_map/reduce_scatter | solution.py:186
  224.5 107.8 %all-gather.22.cloned.1.call-start = ((), (), s32[]{:S(2)}) async-start(), calls=%async_computation.11 | async-start | bytes 1966080 | tf_op jit(solution)/shard_map/all_gather | solution.py:35
  251.6 82.8 %copy-start.4 = (f32[3,512,512]{1,2,0:T(8,128)S(1)}, f32[3,512,512]{1,2,0:T(8,128)}, u32[]{:S(2)}) copy-start(f32[3,512,512]{1,2,0:T(8,128)} %copy-done.3) | copy-start | bytes 9437188
  254.9 107.6 %all-gather.28.cloned.1.call-start = ((), (), s32[]{:S(2)}) async-start(), calls=%async_computation.15 | async-start | bytes 1474560 | tf_op jit(solution)/shard_map/all_gather | solution.py:188
  292.3 109.7 %reduce-scatter.16.cloned.1.call-start = ((), (), s32[]{:S(2)}) async-start(), calls=%async_computation.16 | async-start | bytes 1327104 | tf_op jit(solution)/shard_map/reduce_scatter | solution.py:187
  351.4 92.9 %reduce-scatter.14.cloned.1.call-start = ((), (), s32[]{:S(2)}) async-start(), calls=%async_computation.12 | async-start | bytes 1966080 | tf_op jit(solution)/shard_map/reduce_scatter | solution.py:39
  354.1 135.2 %reduce-scatter.10.cloned.1.call-start = ((), (), s32[]{:S(2)}) async-start(), calls=%async_computation.9 | async-start | bytes 1966080 | tf_op jit(solution)/shard_map/reduce_scatter | solution.py:39
  426.2 63.1 %copy-start.9 = (bf16[256,768]{0,1:T(8,128)(2,1)S(1)}, bf16[256,768]{0,1:T(8,128)(2,1)}, u32[]{:S(2)}) copy-start(bf16[256,768]{0,1:T(8,128)(2,1)} %reduce-scatter.12.cloned.1.call-done) | copy-start | bytes 1179652
  426.2 63.1 %copy-start.10 = (bf16[1,256,768]{1,2,0:T(8,128)(2,1)S(1)}, bf16[1,256,768]{1,2,0:T(8,128)(2,1)}, u32[]{:S(2)}) copy-start(bf16[1,256,768]{1,2,0:T(8,128)(2,1)} %copy.130) | copy-start | bytes 1179652
  426.2 63.1 %copy-start.32 = (f32[256]{0:T(256)S(1)}, f32[256]{0:T(256)}, u32[]{:S(2)}) copy-start(f32[256]{0:T(256)} %broadcast_multiply_fusion.3) | copy-start | bytes 3076
  426.2 63.1 %copy-start.40 = (f32[256]{0:T(256)S(1)}, f32[256]{0:T(256)}, u32[]{:S(2)}) copy-start(f32[256]{0:T(256)} %copy-done.39) | copy-start | bytes 3076
  426.2 63.1 %copy-start.42 = (f32[256]{0:T(256)S(1)}, f32[256]{0:T(256)}, u32[]{:S(2)}) copy-start(f32[256]{0:T(256)} %copy-done.41) | copy-start | bytes 3076
  426.2 63.1 %copy-start.46 = (f32[256]{0:T(256)S(1)}, f32[256]{0:T(256)}, u32[]{:S(2)}) copy-start(f32[256]{0:T(256)} %copy-done.45) | copy-start | bytes 3076
  444.3 48.9 %copy-start.1 = (bf16[384,768]{1,0:T(8,128)(2,1)S(1)}, bf16[384,768]{1,0:T(8,128)(2,1)}, u32[]{:S(2)}) copy-start(bf16[384,768]{1,0:T(8,128)(2,1)} %param.14) | copy-start | bytes 1769476
  (47 other events, 188.3 us)
Sparse Core Ops, SparseCore 0:
  10.2 40.3 all-gather.23
  52.5 22.3 all-gather.15
  77.0 37.0 all-gather.13
  116.4 22.9 all-gather.17
  141.1 24.0 all-gather.19
  166.6 37.0 all-gather.25
  213.3 34.1 reduce-scatter.11
  250.8 41.4 reduce-scatter.17
  294.5 37.6 all-gather.21
  333.8 28.7 all-gather.27
  366.1 35.8 reduce-scatter.15
  404.2 40.0 reduce-scatter.13
  446.6 35.2 reduce-scatter.9
where the time goes:
time: 508 us; the launch traced here: 500 us
  waiting for transfers between devices  278 us (55%)
  blocking collectives  85.8 us (17%)
  matrix products  48.4 us (10%)
  local copies, waits for them, and re-layouts  38.9 us (8%)
  other arithmetic  32.6 us (6%)
  between operations  15.1 us (3%)
    all_gather x3, waiting for transfers between devices, gather_seq(): return lax.all_gather(value, 'seq', axis=0, tiled=True)  92.4 us
    psum x1, blocking collectives, on_device(): norm_sum = lax.psum(norm_terms, ('seq', 'dp'))  41.4 us
    all_gather x1, waiting for transfers between devices, on_device(): context = lax.all_gather(context_here, 'seq', axis=1, tiled=True)  39.3 us
    reduce_scatter x1, waiting for transfers between devices, on_device(): lax.psum_scatter(first_terms, 'dp', scatter_dimension=0, tiled=True)  35.3 us
    reduce_scatter x3, waiting for transfers between devices, scatter_seq(): lax.psum_scatter(value.astype(LOW), 'seq', scatter_dimension=0, tiled=True)  33.9 us
    reduce_scatter x1, waiting for transfers between devices, on_device(): lax.psum_scatter(second_terms, 'dp', scatter_dimension=0, tiled=True)  28.3 us
    all_gather x1, blocking collectives, on_device(): second_all = lax.all_gather(second_sum, 'seq', axis=0)  22.2 us
    all_gather x1, waiting for transfers between devices, on_device(): wide_output = lax.all_gather(output_here, 'dp', axis=0, tiled=True)  21 us
  transfers between devices with their start and end apart: 13, of which 12 were waited for; matrix products, arithmetic and copies ran while one was open for 20% of the time, Pallas kernels for 0%

commit v1 on v0

--- a/solution.py
+++ b/solution.py
@@ -6,6 +6,34 @@
 HEAD_DIM = 64
 LOW = jnp.bfloat16
 F32 = jnp.float32
+
+
+def plan_circles(mine):
+    across = "seq"
+    out_arr = lax.axis_size(across)
+    g_now = lax.axis_index(across)
+    y2, val2, v1 = (out_arr, g_now, mine.shape[1])
+    row_list = []
+    for j, kk in enumerate(mine.shape):
+        row_list.append(kk * y2 if j == 1 else kk)
+    x_next = jnp.zeros(row_list, mine.dtype)
+    finding = lax.dynamic_update_slice_in_dim(x_next, mine, val2 * v1, axis=1)
+    part_next = local_next = mine
+    for ii in tuple(range(1, y2 // 2 + 1)):
+        queue = []
+        for j in tuple(range(y2)):
+            queue.append((j, (j + 1) % y2))
+        part_next = lax.ppermute(part_next, axis_name=across, perm=queue)
+        finding = lax.dynamic_update_slice_in_dim(finding, part_next, (val2 - ii) % y2 * v1, axis=1)
+        if 2 * ii < y2:
+            store = []
+            for j in tuple(range(y2)):
+                store.append((j, (j - 1) % y2))
+            local_next = lax.ppermute(local_next, axis_name=across, perm=store)
+            finding = lax.dynamic_update_slice_in_dim(
+                finding, local_next, (val2 + ii) % y2 * v1, axis=1
+            )
+    return finding
 
 
 def layer_norm(values, gain, bias):
@@ -150,7 +178,7 @@
     keys = projected[:, local_width : 2 * local_width]
     values = projected[:, 2 * local_width :]
     context_here, logs = attention_forward(queries, keys, values)
-    context = lax.all_gather(context_here, "seq", axis=1, tiled=True)
+    context = plan_circles(context_here)
     middle = inputs + matmul(context, wide_proj)
     lowered_two = layer_norm(middle, gain_two, bias_two).astype(LOW)
     hidden_pre = matmul(lowered_two, wide_hidden)

time: 508 us -> 467 us (0.919)
  waiting for transfers between devices: 278 us -> 227 us
  local copies, waits for them, and re-layouts: 38.9 us -> 45.9 us
    all_gather x1 -> x0, waiting for transfers between devices: 39.3 us -> none  [on_device(): context = lax.all_gather(context_here, 'seq', axis=1, tiled=True)]
    ppermute x0 -> x3, waiting for transfers between devices: none -> 20.5 us  [the longest x2 16.5 us: plan_circles(): part_next = lax.ppermute(part_next, axis_name=across, perm=queue)]
    all_gather x1, waiting for transfers between devices: 19.2 us -> 0.01 us  [on_device(): wide_hidden = lax.all_gather(hidden_cols, 'dp', axis=0, tiled=True)]
    all_gather x1, waiting for transfers between devices: 5.78 us -> 0.01 us  [on_device(): wide_proj = lax.all_gather(proj_weight, 'dp', axis=0, tiled=True)]
    dynamic_update_slice x0 -> x3, local copies, waits for them, and re-layouts: none -> 5.33 us  [the longest x2 3.56 us: plan_circles(): lax.dynamic_update_slice_in_dim(finding, part_next, (val2 - ii) % y2 * v1...]
    unnamed x123 -> x127, local copies, waits for them, and re-layouts: 16.8 us -> 16.7 us
  transfers between devices with their start and end apart: 13 -> 15, of which waited for: 12 -> 12; matrix products, arithmetic and copies ran while one was open for 20% -> 24% of each run, Pallas kernels for 0% -> 0%
where the time goes in v1:
time: 467 us; the launch traced here: 462 us
  waiting for transfers between devices  227 us (49%)
  blocking collectives  85 us (18%)
  matrix products  48.9 us (10%)
  local copies, waits for them, and re-layouts  45.9 us (10%)
  other arithmetic  34.1 us (7%)
  between operations  15.5 us (3%)
  starting transfers between devices  5.22 us (1%)
    all_gather x3, waiting for transfers between devices, gather_seq(): return lax.all_gather(value, 'seq', axis=0, tiled=True)  88.7 us
    psum x1, blocking collectives, on_device(): norm_sum = lax.psum(norm_terms, ('seq', 'dp'))  41.2 us
    reduce_scatter x1, waiting for transfers between devices, on_device(): lax.psum_scatter(first_terms, 'dp', scatter_dimension=0, tiled=True)  35.1 us
    reduce_scatter x3, waiting for transfers between devices, scatter_seq(): lax.psum_scatter(value.astype(LOW), 'seq', scatter_dimension=0, tiled=True)  32.9 us
    reduce_scatter x1, waiting for transfers between devices, on_device(): lax.psum_scatter(second_terms, 'dp', scatter_dimension=0, tiled=True)  28.1 us
    all_gather x1, blocking collectives, on_device(): second_all = lax.all_gather(second_sum, 'seq', axis=0)  22.1 us
    all_gather x1, waiting for transfers between devices, on_device(): wide_output = lax.all_gather(output_here, 'dp', axis=0, tiled=True)  20.1 us
    unnamed x127, local copies, waits for them, and re-layouts  16.7 us
  transfers between devices with their start and end apart: 15, of which 12 were waited for; matrix products, arithmetic and copies ran while one was open for 24% of the time, Pallas kernels for 0%

profile of v1, /device:TPU:0, one launch (start us, length us, event | category | flops | bytes accessed | tf_op | source)
XLA Modules:
  0.0 462.0 jit_solution(7412180862958080024)
XLA Ops:
  15.4 10.3 %all-gather.4 = bf16[8,96,4]{1,2,0:T(4,128)(2,1)S(1)} all-gather(bf16[1,96,4]{1,2,0:T(4,128)(2,1)S(1)} %maximum_bitcast_fusion), channel_id=1, replica_groups=mesh['seq'=4,'dp'=8] {'dp'}, dimensions={0}, use_global_device_ids=true | all-gather | bytes 6912 | tf_op jit(solution)/shard_map/all_gather | solution.py:166
  29.0 11.3 %all_gather.38 = bf16[768,576]{1,0:T(8,128)(2,1)S(1)} all-gather(bf16[96,576]{1,0:T(8,128)(2,1)S(1)} %copy.126), channel_id=1, replica_groups=mesh['seq'=4,'dp'=8] {'dp'}, dimensions={0}, use_global_device_ids=true | all-gather | bytes 995328 | tf_op jit(solution)/shard_map/all_gather | solution.py:169
  40.4 10.3 %all-gather.21.cloned.1.call-done = bf16[1,1024,768]{1,2,0:T(8,128)(2,1)} async-done(((bf16[1,256,768]{1,2,0:T(8,128)(2,1)}), bf16[1,1024,768]{1,2,0:T(8,128)(2,1)}) %all-gather.21.cloned.1.call-update) | async-done | bytes 1572880 | tf_op jit(solution)/shard_map/all_gather | solution.py:63
  65.7 3.0 collective-permute-start.1
  68.7 10.3 %collective-permute-done = bf16[1024,192]{0,1:T(8,128)(2,1)} collective-permute-done((bf16[1024,192]{0,1:T(8,128)(2,1)}, bf16[1024,192]{0,1:T(8,128)(2,1)}, u32[]{:S(2)}, u32[]{:S(2)}) %collective-permute-start) | collective-permute-done | bytes 393248 | tf_op jit(solution)/shard_map/ppermute | solution.py:26
  81.5 3.9 collective-permute-done.1
  87.2 6.2 %collective-permute-done.2 = bf16[1024,192]{0,1:T(8,128)(2,1)} collective-permute-done((bf16[1024,192]{0,1:T(8,128)(2,1)}, bf16[1024,192]{0,1:T(8,128)(2,1)}, u32[]{:S(2)}, u32[]{:S(2)}) %collective-permute-start.2) | collective-permute-done | bytes 393248 | tf_op jit(solution)/shard_map/ppermute | solution.py:26
  95.2 3.8 fusion.90
  102.4 4.8 %fusion.91 = f32[1024,768]{1,0:T(8,128)} fusion(bf16[1024,768]{0,1:T(8,128)(2,1)} %add_convert_fusion, bf16[768,768]{1,0:T(8,128)(2,1)} %all-gather.15.cloned.1.call-done), kind=kOutput, calls=%fused_computation.170 | convolution fusion | flops 1207959552 | bytes 5898240 | tf_op jit(solution)/shard_map/dot_general | solution.py:51
  107.2 20.1 %all-gather.17.cloned.1.call-done = bf16[768,768]{1,0:T(8,128)(2,1)} async-done(((bf16[96,768]{1,0:T(8,128)(2,1)}), bf16[768,768]{1,0:T(8,128)(2,1)}) %all-gather.17.cloned.1.call-update) | async-done | bytes 1179664 | tf_op jit(solution)/shard_map/all_gather | solution.py:172
  127.3 38.5 %all-gather.23.cloned.1.call-done = bf16[1,1024,768]{2,1,0:T(8,128)(2,1)} async-done(((bf16[1,256,768]{2,1,0:T(8,128)(2,1)}), bf16[1,1024,768]{2,1,0:T(8,128)(2,1)}) %all-gather.23.cloned.1.call-update) | async-done | bytes 1572880 | tf_op jit(solution)/shard_map/all_gather | solution.py:63
  165.8 5.6 %fusion.16 = bf16[1024,768]{1,0:T(8,128)(2,1)S(1)} fusion(f32[1024,768]{1,0:T(8,128)} %fusion.91, bf16[768,768]{1,0:T(8,128)(2,1)} %all-gather.17.cloned.1.call-done, bf16[1,1024,768]{2,1,0:T(8,128)(2,1)} %all-gather.23.cloned.1.call-done), kind=kOutput, calls=%fused_computation.26 | convolution fusion | flops 1223688192 | bytes 7471104 | tf_op jit(solution)/shard_map/dot_general | solution.py:59
  175.2 3.5 convolution_convert_fusion.3
  182.0 4.3 copy.156
  190.3 19.2 %reduce-scatter.12.cloned.1.call-done = bf16[256,768]{0,1:T(8,128)(2,1)} async-done(((bf16[1024,768]{0,1:T(8,128)(2,1)}), bf16[256,768]{0,1:T(8,128)(2,1)}) %reduce-scatter.12.cloned.1.call-update) | async-done | bytes 393232 | tf_op jit(solution)/shard_map/reduce_scatter | solution.py:67
  219.2 35.1 %reduce-scatter.18.cloned.1.call-done = bf16[96,1536]{1,0:T(8,128)(2,1)} async-done(((bf16[768,1536]{1,0:T(8,128)(2,1)}), bf16[96,1536]{1,0:T(8,128)(2,1)}) %reduce-scatter.18.cloned.1.call-update) | async-done | bytes 294928 | tf_op jit(solution)/shard_map/reduce_scatter | solution.py:214
  254.4 39.9 %all-gather.19.cloned.1.call-done = bf16[1024,768]{0,1:T(8,128)(2,1)} async-done(((bf16[256,768]{0,1:T(8,128)(2,1)}), bf16[1024,768]{0,1:T(8,128)(2,1)}) %all-gather.19.cloned.1.call-update) | async-done | bytes 1572880 | tf_op jit(solution)/shard_map/all_gather | solution.py:63
  316.5 5.0 %convolution_convert_fusion.2 = bf16[1024,768]{0,1:T(8,128)(2,1)} fusion(bf16[768,768]{1,0:T(8,128)(2,1)} %all-gather.17.cloned.1.call-done, f32[1024,768]{1,0:T(8,128)} %fusion.91), kind=kOutput, calls=%fused_computation.50 | convolution fusion | flops 1215823872 | bytes 5898240 | tf_op jit(solution)/shard_map/dot_general | solution.py:51
  331.1 3.6 reshape.282
  335.9 28.1 %reduce-scatter.16.cloned.1.call-done = bf16[96,768]{1,0:T(8,128)(2,1)} async-done(((bf16[768,768]{1,0:T(8,128)(2,1)}), bf16[96,768]{1,0:T(8,128)(2,1)}) %reduce-scatter.16.cloned.1.call-update) | async-done | bytes 147472 | tf_op jit(solution)/shard_map/reduce_scatter | solution.py:215
  364.0 22.1 %all-gather.2 = bf16[384,768]{1,0:T(8,128)(2,1)S(1)} all-gather(bf16[96,768]{1,0:T(8,128)(2,1)} %reduce-scatter.16.cloned.1.call-done), channel_id=4, replica_groups=mesh['seq'=4,'dp'=8] {'seq'}, dimensions={0}, use_global_device_ids=true | all-gather | bytes 737280 | tf_op jit(solution)/shard_map/all_gather | solution.py:217
  389.6 2.9 reshape.280
  392.6 13.7 %reduce-scatter.14.cloned.1.call-done = bf16[256,768]{0,1:T(8,128)(2,1)} async-done(((bf16[1024,768]{0,1:T(8,128)(2,1)}), bf16[256,768]{0,1:T(8,128)(2,1)}) %reduce-scatter.14.cloned.1.call-update) | async-done | bytes 393232 | tf_op jit(solution)/shard_map/reduce_scatter | solution.py:67
  409.3 41.2 %psum.7 = f32[4,768]{1,0:T(4,128)S(1)} all-reduce(f32[4,768]{1,0:T(4,128)S(1)} %pad_maximum_fusion.6), channel_id=1, replica_groups=mesh['seq'=4,'dp'=8] {'seq','dp'}, use_global_device_ids=true, to_apply=%region_27.28 | all-reduce | flops 3072 | bytes 24576 | tf_op jit(solution)/shard_map/psum | solution.py:237
  (247 shorter events, 99.6 us)
Async XLA Ops:
  7.2 43.4 %all-gather.21.cloned.1.call-start = ((), (), s32[]{:S(2)}) async-start(), calls=%async_computation.12 | async-start | bytes 1966080 | tf_op jit(solution)/shard_map/all_gather | solution.py:63
  9.3 85.9 %all-gather.13.cloned.1.call-start = ((), (), s32[]{:S(2)}) async-start(), calls=%async_computation.5 | async-start | bytes 1327104 | tf_op jit(solution)/shard_map/all_gather | solution.py:170
  10.1 92.3 %all-gather.15.cloned.1.call-start = ((), (), s32[]{:S(2)}) async-start(), calls=%async_computation.6 | async-start | bytes 1327104 | tf_op jit(solution)/shard_map/all_gather | solution.py:171
  14.5 112.7 %all-gather.17.cloned.1.call-start = ((), (), s32[]{:S(2)}) async-start(), calls=%async_computation.7 | async-start | bytes 1327104 | tf_op jit(solution)/shard_map/all_gather | solution.py:172
  15.3 150.5 %all-gather.23.cloned.1.call-start = ((), (), s32[]{:S(2)}) async-start(), calls=%async_computation.13 | async-start | bytes 1966080 | tf_op jit(solution)/shard_map/all_gather | solution.py:63
  26.5 27.9 %copy-start.46 = (f32[768]{0:T(1024)}, f32[768]{0:T(1024)S(1)}, u32[]{:S(2)}) copy-start(f32[768]{0:T(1024)S(1)} %get-tuple-element.82) | copy-start | bytes 9220
  64.9 14.2 %collective-permute-start = (bf16[1024,192]{0,1:T(8,128)(2,1)}, bf16[1024,192]{0,1:T(8,128)(2,1)}, u32[]{:S(2)}, u32[]{:S(2)}) collective-permute-start(bf16[1024,192]{0,1:T(8,128)(2,1)} %get-tuple-element.96), channel_id=1, source_target_pairs={{0,8},{8,16},{16,24},{24,0},{1,9},{9,17},{17,25},{25,1},{2,10},{10... | collective-permute-start | bytes 1179656 | tf_op jit(solution)/shard_map/ppermute | solution.py:26
  65.7 19.7 %collective-permute-start.1 = (bf16[1024,192]{0,1:T(8,128)(2,1)}, bf16[1024,192]{0,1:T(8,128)(2,1)}, u32[]{:S(2)}, u32[]{:S(2)}) collective-permute-start(bf16[1024,192]{0,1:T(8,128)(2,1)} %get-tuple-element.96), channel_id=1, source_target_pairs={{0,24},{8,0},{16,8},{24,16},{1,25},{9,1},{17,9},{25,17},{2,26},{10... | collective-permute-start | bytes 1179656 | tf_op jit(solution)/shard_map/ppermute | solution.py:32
  79.1 14.3 %collective-permute-start.2 = (bf16[1024,192]{0,1:T(8,128)(2,1)}, bf16[1024,192]{0,1:T(8,128)(2,1)}, u32[]{:S(2)}, u32[]{:S(2)}) collective-permute-start(bf16[1024,192]{0,1:T(8,128)(2,1)} %collective-permute-done), channel_id=1, source_target_pairs={{0,8},{8,16},{16,24},{24,0},{1,9},{9,17},{17,25},{25,1},{2,10},{10... | collective-permute-start | bytes 1179656 | tf_op jit(solution)/shard_map/ppermute | solution.py:26
  79.1 130.4 %reduce-scatter.12.cloned.1.call-start = ((), (), s32[]{:S(2)}) async-start(), calls=%async_computation.9 | async-start | bytes 1966080 | tf_op jit(solution)/shard_map/reduce_scatter | solution.py:67
  175.1 79.2 %reduce-scatter.18.cloned.1.call-start = ((), (), s32[]{:S(2)}) async-start(), calls=%async_computation.16 | async-start | bytes 2654208 | tf_op jit(solution)/shard_map/reduce_scatter | solution.py:214
  186.3 108.0 %all-gather.19.cloned.1.call-start = ((), (), s32[]{:S(2)}) async-start(), calls=%async_computation.10 | async-start | bytes 1966080 | tf_op jit(solution)/shard_map/all_gather | solution.py:63
  217.1 107.5 %all-gather.25.cloned.1.call-start = ((), (), s32[]{:S(2)}) async-start(), calls=%async_computation.14 | async-start | bytes 1474560 | tf_op jit(solution)/shard_map/all_gather | solution.py:216
  254.3 109.6 %reduce-scatter.16.cloned.1.call-start = ((), (), s32[]{:S(2)}) async-start(), calls=%async_computation.15 | async-start | bytes 1327104 | tf_op jit(solution)/shard_map/reduce_scatter | solution.py:215
  313.6 92.6 %reduce-scatter.14.cloned.1.call-start = ((), (), s32[]{:S(2)}) async-start(), calls=%async_computation.11 | async-start | bytes 1966080 | tf_op jit(solution)/shard_map/reduce_scatter | solution.py:67
  316.2 134.8 %reduce-scatter.10.cloned.1.call-start = ((), (), s32[]{:S(2)}) async-start(), calls=%async_computation.8 | async-start | bytes 1966080 | tf_op jit(solution)/shard_map/reduce_scatter | solution.py:67
  388.0 21.2 %copy-start.42 = (f32[1,768]{1,0:T(1,128)S(1)}, f32[1,768]{1,0:T(1,128)}, u32[]{:S(2)}) copy-start(f32[1,768]{1,0:T(1,128)} %reshape.279) | copy-start | bytes 9220
  388.0 63.1 %copy-start.7 = (bf16[256,768]{0,1:T(8,128)(2,1)S(1)}, bf16[256,768]{0,1:T(8,128)(2,1)}, u32[]{:S(2)}) copy-start(bf16[256,768]{0,1:T(8,128)(2,1)} %reduce-scatter.12.cloned.1.call-done) | copy-start | bytes 1179652
  388.0 63.1 %copy-start.8 = (bf16[1,256,768]{1,2,0:T(8,128)(2,1)S(1)}, bf16[1,256,768]{1,2,0:T(8,128)(2,1)}, u32[]{:S(2)}) copy-start(bf16[1,256,768]{1,2,0:T(8,128)(2,1)} %copy.130) | copy-start | bytes 1179652
  388.0 63.1 %copy-start.31 = (f32[256]{0:T(256)S(1)}, f32[256]{0:T(256)}, u32[]{:S(2)}) copy-start(f32[256]{0:T(256)} %broadcast_multiply_fusion.3) | copy-start | bytes 3076
  388.0 63.1 %copy-start.39 = (f32[256]{0:T(256)S(1)}, f32[256]{0:T(256)}, u32[]{:S(2)}) copy-start(f32[256]{0:T(256)} %copy-done.38) | copy-start | bytes 3076
  388.0 63.1 %copy-start.41 = (f32[256]{0:T(256)S(1)}, f32[256]{0:T(256)}, u32[]{:S(2)}) copy-start(f32[256]{0:T(256)} %copy-done.40) | copy-start | bytes 3076
  388.0 63.1 %copy-start.45 = (f32[256]{0:T(256)S(1)}, f32[256]{0:T(256)}, u32[]{:S(2)}) copy-start(f32[256]{0:T(256)} %copy-done.44) | copy-start | bytes 3076
  406.2 48.7 %copy-start.1 = (bf16[384,768]{1,0:T(8,128)(2,1)S(1)}, bf16[384,768]{1,0:T(8,128)(2,1)}, u32[]{:S(2)}) copy-start(bf16[384,768]{1,0:T(8,128)(2,1)} %param.14) | copy-start | bytes 1769476
  (51 other events, 237.6 us)
Sparse Core Ops, SparseCore 0:
  10.2 40.3 all-gather.20
  52.5 22.2 all-gather.12
  77.3 24.0 all-gather.14
  103.2 24.0 all-gather.16
  128.7 37.0 all-gather.22
  175.3 34.1 reduce-scatter.11
  212.8 41.4 reduce-scatter.17
  256.5 37.6 all-gather.18
  295.9 28.6 all-gather.24
  328.0 35.8 reduce-scatter.15
  366.3 39.8 reduce-scatter.13
  408.4 35.1 reduce-scatter.9
